TPU v7x, 32 devices: a whole 2x2x4 slice. The times are simulated.
32 devices in a mesh: grp: 2 (over y), gx: 4 (over z), gy: 4 (over x, core).
Axes of the slice: x: 2, y: 2, z: 4, core: 2. Of those that a mesh axis runs over, the one named last changes fastest.
Arguments:
- counts: int32 [256, 256, 256], P(('grp', 'gx'), 'gy'), parts along dimension 0, may hold values from -40 to 999
Outputs:
- denoised: float32 [256, 256, 256], P(('grp', 'gx'), 'gy'), parts along dimension 0
There are 2 independent parts, one for each index of `grp`. A program takes and returns all parts, laid end to end along the dimension named above; each array names one. Nothing has to cross between parts.
All inputs are finite; a program needn't handle non-finite values.
Results may differ from a plain program's by a relative error of at most 0.00005.
Values sent between devices are 32-bit elements; how exact they have to be, the bound alone decides.
A program may use at most 64 MiB of HBM per device.

v0:
```python
import functools
import math

import jax
import jax.numpy as jnp
import ml_dtypes
import numpy as np
from jax import lax
from jax.experimental import pallas as pl
from jax.experimental.pallas import tpu as pltpu
from jax.sharding import PartitionSpec as P

ROOT_THREE = math.sqrt(3.0)
TAP_SCALE = 4.0 * math.sqrt(2.0)
H = [
    (1.0 + ROOT_THREE) / TAP_SCALE,
    (3.0 + ROOT_THREE) / TAP_SCALE,
    (3.0 - ROOT_THREE) / TAP_SCALE,
    (1.0 - ROOT_THREE) / TAP_SCALE,
]
G = [H[3], -H[2], H[1], -H[0]]
THRESHOLD = 0.1
MESH = pl.DeviceIdType.MESH
F32 = jnp.float32
BF16 = jnp.bfloat16


def split_matrix(matrix):
    high = matrix.astype(ml_dtypes.bfloat16)
    low = (matrix - high.astype(np.float32)).astype(ml_dtypes.bfloat16)
    return np.stack([high, low])


def time_matrices(length, padded):
    matrix = np.zeros((padded, padded), np.float32)
    for k in range(length // 2):
        for j in range(4):
            matrix[(2 * k + j) % length, k] += H[j]
            matrix[(2 * k + j) % length, length // 2 + k] += G[j]
    return split_matrix(matrix), split_matrix(np.ascontiguousarray(matrix.T))


def times(values, matrix_ref):
    high = values.astype(BF16)
    low = (values - high.astype(F32)).astype(BF16)
    first = matrix_ref[0]
    second = matrix_ref[1]
    dot = functools.partial(jnp.dot, preferred_element_type=F32)
    return dot(high, first) + (dot(low, first) + dot(high, second))


def shrink(values):
    return values - jnp.clip(values, -THRESHOLD, THRESHOLD)


def low_of(e):
    return (H[0] * e[0] + H[1] * e[1]) + (H[2] * e[2] + H[3] * e[3])


def high_of(e):
    return (G[0] * e[0] + G[1] * e[1]) + (G[2] * e[2] + G[3] * e[3])


def even_of(lo, hi, lo_before, hi_before):
    return (H[0] * lo + G[0] * hi) + (H[2] * lo_before + G[2] * hi_before)


def odd_of(lo, hi, lo_before, hi_before):
    return (H[1] * lo + G[1] * hi) + (H[3] * lo_before + G[3] * hi_before)


def loop(count, body, unroll=1):
    def step(i, carry):
        body(i)
        return carry

    lax.fori_loop(0, count, step, 0, unroll=unroll)


def rows(start, size):
    return pl.ds(pl.multiple_of(start, 8), size)


def kernel(
    nx, ny,
    counts, m1, m1t, m2, m2t, m3, m3t, out,
    t0, a0, c1, e1, t2, a2, c2, e2, t3, a3, c3,
    s3, p3, d2, s2, p2, d1, s1, p1, reb, edge,
    f0x, f0y, f0c, f0xr, f0yr, f0cr,
    f1x, f1y, f1c, f1xr, f1yr, f1cr,
    i1x, i1y, i1c, i1xr, i1yr, i1cr,
    i2x, i2y, i2c, i2xr, i2yr, i2cr,
    send_sem, recv_sem,
):
    gx = lax.axis_index("gx")
    gy = lax.axis_index("gy")
    x_after, x_before = lax.rem(gx + 1, nx), lax.rem(gx + nx - 1, nx)
    y_after, y_before = lax.rem(gy + 1, ny), lax.rem(gy + ny - 1, ny)
    before = [{"gx": x_before}, {"gy": y_before}, {"gx": x_before, "gy": y_before}]
    after = [{"gx": x_after}, {"gy": y_after}, {"gx": x_after, "gy": y_after}]

    barrier = pltpu.get_barrier_semaphore()
    for other in before + after:
        pl.semaphore_signal(barrier, inc=1, device_id=other, device_id_type=MESH)

    def send(round_no, sources, targets, others):
        copies = []
        for n in range(3):
            copy = pltpu.make_async_remote_copy(
                src_ref=sources[n],
                dst_ref=targets[n],
                send_sem=send_sem.at[3 * round_no + n],
                recv_sem=recv_sem.at[3 * round_no + n],
                device_id=others[n],
                device_id_type=MESH,
            )
            copy.start()
            copies.append(copy)
        return copies

    def wait(copies):
        for copy in copies:
            copy.wait()

    def residual(count, rebuilt):
        observed = count.astype(F32) * (1.0 / 64.0)
        weight = 1.0 / (1.0 + jnp.abs(observed))
        if rebuilt is None:
            return weight * observed
        return weight * (observed - rebuilt)

    def iteration(number):
        first = number == 0

        def old(ref, *index):
            return 0.0 if first else ref[index]

        for i in range(2):
            for th in range(2):
                f0x[th, i * 64 : (i + 1) * 64, :] = residual(
                    counts[i, :, th * 128 : (th + 1) * 128],
                    None if first else reb[th, i * 64 : (i + 1) * 64, :],
                )

        def edge_row(x):
            for th in range(2):
                edge[th, rows(x * 8, 8), :] = residual(
                    counts[x, 0:8, th * 128 : (th + 1) * 128],
                    None if first else reb[th, rows(x * 64, 8), :],
                )

        loop(32, edge_row, unroll=4)
        for th in range(2):
            for j in range(2):
                f0y[th, j * 32 : (j + 1) * 32, :] = edge[th, pl.ds(j, 32, stride=8), :]
            for i in range(2):
                f0c[th, i * 8 : (i + 1) * 8, :] = f0x[th, i * 64 : i * 64 + 8, :]
        if first:
            pl.semaphore_wait(barrier, 6)
        f0 = send(4 * number, [f0x, f0y, f0c], [f0xr, f0yr, f0cr], before)

        def time_rows(n):
            count = counts[pl.ds(n * 4, 4)].reshape(256, 256)
            if first:
                values = residual(count, None)
            else:
                rebuilt = jnp.concatenate(
                    [reb[0, rows(n * 256, 256), :], reb[1, rows(n * 256, 256), :]], axis=1
                )
                values = residual(count, rebuilt)
            result = times(values, m1)
            for i in range(4):
                for tb in range(2):
                    t0[tb, rows((n * 4 + i) * 72, 64), :] = result[
                        i * 64 : (i + 1) * 64, tb * 128 : (tb + 1) * 128
                    ]

        loop(8, time_rows)
        wait(f0)
        result = times(jnp.concatenate([f0xr[0], f0xr[1]], axis=1), m1)
        for i in range(2):
            for tb in range(2):
                t0[tb, (32 + i) * 72 : (32 + i) * 72 + 64, :] = result[
                    i * 64 : (i + 1) * 64, tb * 128 : (tb + 1) * 128
                ]
        result = times(jnp.concatenate([f0yr[0], f0yr[1]], axis=1), m1)
        for j in range(2):
            for tb in range(2):
                t0[tb, pl.ds(64 + j, 32, stride=72), :] = result[
                    j * 32 : (j + 1) * 32, tb * 128 : (tb + 1) * 128
                ]
        result = times(jnp.concatenate([f0cr[0], f0cr[1]], axis=1), m1)
        for i in range(2):
            for tb in range(2):
                t0[tb, (32 + i) * 72 + 64 : (33 + i) * 72, :] = result[
                    i * 8 : (i + 1) * 8, tb * 128 : (tb + 1) * 128
                ]

        def x_level1(k):
            for tb in range(2):
                e = [t0[tb, rows((2 * k + j) * 72, 72), :] for j in range(4)]
                a0[tb, rows(k * 72, 72), :] = low_of(e)
                a0[2 + tb, rows(k * 72, 72), :] = high_of(e)

        loop(16, x_level1)

        def y_level1(k):
            for xb in range(2):
                for tb in range(2):
                    e = [a0[2 * xb + tb, pl.ds(k * 72 + j, 32, stride=2), :] for j in range(4)]
                    for yb in range(2):
                        value = high_of(e) if yb else low_of(e)
                        band = 4 * xb + 2 * yb + tb
                        if band == 0:
                            e1[rows(k * 40, 32), :] = value
                        else:
                            place = rows((k + 1) * 40 + 8, 32)
                            c1[band - 1, place, :] = shrink(old(c1, band - 1, place, slice(None)) + value)

        loop(16, y_level1)

        for i in range(6):
            f1x[i * 32 : (i + 1) * 32, :] = e1[i * 40 : i * 40 + 32, :]
            f1c[i * 8 : (i + 1) * 8, :] = e1[i * 40 : i * 40 + 8, :]
            f1y[i * 16 : (i + 1) * 16, :] = e1[pl.ds(i, 16, stride=40), :]
        f1 = send(4 * number + 1, [f1x, f1y, f1c], [f1xr, f1yr, f1cr], before)
        for b in range(7):
            i1x[b * 32 : (b + 1) * 32, :] = c1[b, 16 * 40 + 8 : 17 * 40, :]
            i1y[b * 16 : (b + 1) * 16, :] = c1[b, pl.ds(40 + 39, 16, stride=40), :]
            i1c[b * 8 : (b + 1) * 8, :] = c1[b, 16 * 40 + 32 : 17 * 40, :]
        i1 = send(4 * number + 2, [i1x, i1y, i1c], [i1xr, i1yr, i1cr], after)
        wait(f1)
        for i in range(6):
            e1[(16 + i) * 40 : (16 + i) * 40 + 32, :] = f1xr[i * 32 : (i + 1) * 32, :]
            e1[(16 + i) * 40 + 32 : (17 + i) * 40, :] = f1cr[i * 8 : (i + 1) * 8, :]
            e1[pl.ds(32 + i, 16, stride=40), :] = f1yr[i * 16 : (i + 1) * 16, :]

        def time_level2(n):
            t2[rows(n * 176, 176), :] = times(e1[rows(n * 176, 176), :], m2)

        loop(5, time_level2)

        def x_level2(k):
            e = [t2[rows((2 * k + j) * 40, 40), :] for j in range(4)]
            a2[0, rows(k * 40, 40), :] = low_of(e)
            a2[1, rows(k * 40, 40), :] = high_of(e)

        loop(10, x_level2)

        def y_level2_low(k):
            e = [a2[0, pl.ds(k * 40 + j, 18, stride=2), :] for j in range(4)]
            e2[rows(k * 24, 18), :] = low_of(e)

        loop(10, y_level2_low)

        def y_level2(k):
            place = rows((k + 2) * 24 + 8, 16)
            for xb in range(2):
                e = [a2[xb, pl.ds(k * 40 + j, 16, stride=2), :] for j in range(4)]
                for yb in range(2):
                    value = high_of(e) if yb else low_of(e)
                    b = 2 * xb + yb
                    c2[b, place, :] = shrink(old(c2, b, place, slice(None)) + value)

        loop(8, y_level2)

        t3[...] = times(e2[...], m3)

        def x_level3(k):
            e = [t3[rows((2 * k + j) * 24, 24), :] for j in range(4)]
            a3[0, rows(k * 24, 24), :] = low_of(e)
            a3[1, rows(k * 24, 24), :] = high_of(e)

        loop(4, x_level3)

        lane = lax.broadcasted_iota(jnp.int32, (8, 128), 1)

        def y_level3(k):
            place = rows((k + 2) * 16 + 8, 8)
            for xb in range(2):
                e = [a3[xb, pl.ds(k * 24 + j, 8, stride=2), :] for j in range(4)]
                for yb in range(2):
                    value = high_of(e) if yb else low_of(e)
                    b = 2 * xb + yb
                    value = old(c3, b, place, slice(None)) + value
                    if b == 0:
                        c3[b, place, :] = jnp.where(lane < 32, value, shrink(value))
                    else:
                        c3[b, place, :] = shrink(value)

        loop(4, y_level3)

        for b in range(4):
            for i in range(2):
                n = 2 * b + i
                i2x[n * 16 : (n + 1) * 16, :] = c2[b, (8 + i) * 24 + 8 : (9 + i) * 24, :]
                i2x[128 + n * 8 : 128 + (n + 1) * 8, :] = c3[b, (4 + i) * 16 + 8 : (5 + i) * 16, :]
                i2y[n * 8 : (n + 1) * 8, :] = c2[b, pl.ds(2 * 24 + 22 + i, 8, stride=24), :]
                i2y[64 + n * 4 : 64 + (n + 1) * 4, :] = c3[b, pl.ds(2 * 16 + 14 + i, 4, stride=16), :]
                i2c[n * 8 : (n + 1) * 8, :] = c2[b, (8 + i) * 24 + 16 : (9 + i) * 24, :]
                i2c[64 + n * 8 : 64 + (n + 1) * 8, :] = c3[b, (4 + i) * 16 + 8 : (5 + i) * 16, :]
        i2 = send(4 * number + 3, [i2x, i2y, i2c], [i2xr, i2yr, i2cr], after)
        wait(i2)
        for b in range(4):
            for i in range(2):
                n = 2 * b + i
                c2[b, i * 24 + 8 : (i + 1) * 24, :] = i2xr[n * 16 : (n + 1) * 16, :]
                c3[b, i * 16 + 8 : (i + 1) * 16, :] = i2xr[128 + n * 8 : 128 + (n + 1) * 8, :]
                c2[b, pl.ds(2 * 24 + 6 + i, 8, stride=24), :] = i2yr[n * 8 : (n + 1) * 8, :]
                c3[b, pl.ds(2 * 16 + 6 + i, 4, stride=16), :] = i2yr[64 + n * 4 : 64 + (n + 1) * 4, :]
                c2[b, i * 24 : i * 24 + 8, :] = i2cr[n * 8 : (n + 1) * 8, :]
                c3[b, i * 16 : i * 16 + 8, :] = i2cr[64 + n * 8 : 64 + (n + 1) * 8, :]

        for b in range(4):
            s3[b] = times(c3[b], m3t)

        def x_up3(k):
            for yb in range(2):
                e = [s3[b, rows((k + d) * 16, 16), :] for d in (1, 0) for b in (yb, 2 + yb)]
                p3[yb, rows(2 * k * 16, 16), :] = even_of(*e)
                p3[yb, rows((2 * k + 1) * 16, 16), :] = odd_of(*e)

        loop(5, x_up3)

        def y_up3(r):
            e = [p3[b, pl.ds(r * 16 + d, 9), :] for d in (7, 6) for b in (0, 1)]
            d2[pl.ds(r * 24 + 6, 9, stride=2), :] = even_of(*e)
            d2[pl.ds(r * 24 + 7, 9, stride=2), :] = odd_of(*e)

        loop(10, y_up3)

        lanes = lax.broadcasted_iota(jnp.int32, (240, 128), 1)
        s2[0] = times(jnp.where(lanes < 64, d2[...], c2[0]), m2t)
        for b in range(1, 4):
            s2[b] = times(c2[b], m2t)

        def x_up2(k):
            for yb in range(2):
                e = [s2[b, rows((k + d) * 24, 24), :] for d in (1, 0) for b in (yb, 2 + yb)]
                p2[yb, rows(2 * k * 24, 24), :] = even_of(*e)
                p2[yb, rows((2 * k + 1) * 24, 24), :] = odd_of(*e)

        loop(9, x_up2)

        def y_up2(r):
            e = [p2[b, pl.ds(r * 24 + d, 17), :] for d in (7, 6) for b in (0, 1)]
            d1[pl.ds(r * 40 + 6, 17, stride=2), :] = even_of(*e)
            d1[pl.ds(r * 40 + 7, 17, stride=2), :] = odd_of(*e)

        loop(18, y_up2)

        wait(i1)
        for b in range(7):
            c1[b, 8:40, :] = i1xr[b * 32 : (b + 1) * 32, :]
            c1[b, pl.ds(40 + 7, 16, stride=40), :] = i1yr[b * 16 : (b + 1) * 16, :]
            c1[b, 0:8, :] = i1cr[b * 8 : (b + 1) * 8, :]

        def time_up1(n):
            place = rows(n * 136, 136)
            for b in range(4):
                lo = d1[rows(40 + n * 136, 136), :] if b == 0 else c1[2 * b - 1, place, :]
                values = jnp.concatenate([lo, c1[2 * b, place, :]], axis=1)
                result = times(values, m1t)
                s1[0, b, place, :] = result[:, :128]
                s1[1, b, place, :] = result[:, 128:]

        loop(5, time_up1)

        def x_up1(k):
            for th in range(2):
                for yb in range(2):
                    e = [s1[th, b, rows((k + d) * 40, 40), :] for d in (1, 0) for b in (yb, 2 + yb)]
                    p1[th, yb, rows(2 * k * 40, 40), :] = even_of(*e)
                    p1[th, yb, rows((2 * k + 1) * 40, 40), :] = odd_of(*e)

        loop(16, x_up1)

        def y_up1(r):
            for th in range(2):
                e = [p1[th, b, pl.ds(r * 40 + d, 32), :] for d in (8, 7) for b in (0, 1)]
                reb[th, pl.ds(r * 64, 32, stride=2), :] = even_of(*e)
                reb[th, pl.ds(r * 64 + 1, 32, stride=2), :] = odd_of(*e)

        loop(32, y_up1)

    iteration(0)
    iteration(1)

    def finish(r):
        for th in range(2):
            out[r, :, th * 128 : (th + 1) * 128] = reb[th, rows(r * 64, 64), :]

    loop(32, finish, unroll=2)


def solution(mesh):
    nx, ny = mesh.shape["gx"], mesh.shape["gy"]
    m1, m1t = time_matrices(256, 256)
    m2, m2t = time_matrices(128, 128)
    m3, m3t = time_matrices(64, 128)

    def v(*shape):
        return pltpu.VMEM(shape, F32)

    scratch = [
        v(2, 34 * 72, 128), v(4, 16 * 72, 128), v(7, 17 * 40, 128), v(22 * 40, 128),
        v(22 * 40, 128), v(2, 10 * 40, 128), v(4, 10 * 24, 128), v(10 * 24, 128),
        v(10 * 24, 128), v(2, 4 * 24, 128), v(4, 6 * 16, 128),
        v(4, 6 * 16, 128), v(2, 10 * 16, 128), v(10 * 24, 128),
        v(4, 10 * 24, 128), v(2, 18 * 24, 128), v(18 * 40, 128),
        v(2, 4, 17 * 40, 128), v(2, 2, 32 * 40, 128), v(2, 32 * 64, 128), v(2, 32 * 8, 128),
    ]
    for shapes in (
        ((2, 128, 128), (2, 64, 128), (2, 16, 128)),
        ((192, 128), (96, 128), (48, 128)),
        ((224, 128), (112, 128), (56, 128)),
        ((192, 128), (96, 128), (128, 128)),
    ):
        scratch += [v(*shape) for shape in shapes] * 2
    scratch += [pltpu.SemaphoreType.DMA((24,)), pltpu.SemaphoreType.DMA((24,))]

    def on_device(counts):
        return pl.pallas_call(
            functools.partial(kernel, nx, ny),
            out_shape=jax.ShapeDtypeStruct(counts.shape, F32),
            in_specs=[pl.BlockSpec(memory_space=pltpu.VMEM)] * 7,
            out_specs=pl.BlockSpec(memory_space=pltpu.VMEM),
            scratch_shapes=scratch,
            compiler_params=pltpu.CompilerParams(
                collective_id=0, has_side_effects=True, vmem_limit_bytes=48 * 1024 * 1024
            ),
        )(counts, m1, m1t, m2, m2t, m3, m3t)

    spec = P(("grp", "gx"), "gy", None)
    return jax.shard_map(on_device, mesh=mesh, in_specs=(spec,), out_specs=spec, check_vma=False)
```

profile of v0, /device:TPU:0, one launch (start us, length us, event | category | flops | bytes accessed | tf_op | source)
XLA Modules:
  0.0 64.7 jit_solution(10320485141989794260)
XLA Ops:
  0.0 0.0 copy-start
  0.0 1.6 %copy-done = s32[32,64,256]{2,1,0:T(8,128)S(1)} copy-done((s32[32,64,256]{2,1,0:T(8,128)S(1)}, s32[32,64,256]{2,1,0:T(8,128)}, u32[]{:S(2)}) %copy-start) | copy-done | bytes 2097176
  1.6 0.0 copy-start.1
  1.6 0.9 %copy-done.1 = bf16[2,256,256]{2,1,0:T(8,128)(2,1)S(1)} copy-done((bf16[2,256,256]{2,1,0:T(8,128)(2,1)S(1)}, bf16[2,256,256]{2,1,0:T(8,128)(2,1)}, u32[]{:S(2)}) %copy-start.1) | copy-done | bytes 262168
  2.5 0.0 copy-start.2
  2.5 0.9 %copy-done.2 = bf16[2,256,256]{2,1,0:T(8,128)(2,1)S(1)} copy-done((bf16[2,256,256]{2,1,0:T(8,128)(2,1)S(1)}, bf16[2,256,256]{2,1,0:T(8,128)(2,1)}, u32[]{:S(2)}) %copy-start.2) | copy-done | bytes 262168
  3.5 0.0 copy-start.3
  3.5 0.8 %copy-done.3 = bf16[2,128,128]{2,1,0:T(8,128)(2,1)S(1)} copy-done((bf16[2,128,128]{2,1,0:T(8,128)(2,1)S(1)}, bf16[2,128,128]{2,1,0:T(8,128)(2,1)}, u32[]{:S(2)}) %copy-start.3) | copy-done | bytes 65560
  4.3 0.0 copy-start.4
  4.3 0.8 %copy-done.4 = bf16[2,128,128]{2,1,0:T(8,128)(2,1)S(1)} copy-done((bf16[2,128,128]{2,1,0:T(8,128)(2,1)S(1)}, bf16[2,128,128]{2,1,0:T(8,128)(2,1)}, u32[]{:S(2)}) %copy-start.4) | copy-done | bytes 65560
  5.2 0.0 copy-start.5
  5.2 0.8 %copy-done.5 = bf16[2,128,128]{2,1,0:T(8,128)(2,1)S(1)} copy-done((bf16[2,128,128]{2,1,0:T(8,128)(2,1)S(1)}, bf16[2,128,128]{2,1,0:T(8,128)(2,1)}, u32[]{:S(2)}) %copy-start.5) | copy-done | bytes 65560
  6.0 0.0 copy-start.6
  6.0 0.8 %copy-done.6 = bf16[2,128,128]{2,1,0:T(8,128)(2,1)S(1)} copy-done((bf16[2,128,128]{2,1,0:T(8,128)(2,1)S(1)}, bf16[2,128,128]{2,1,0:T(8,128)(2,1)}, u32[]{:S(2)}) %copy-start.6) | copy-done | bytes 65560
  6.9 56.5 %shard_map.73 = f32[32,64,256]{2,1,0:T(8,128)S(1)} custom-call(s32[32,64,256]{2,1,0:T(8,128)S(1)} %copy-done, bf16[2,256,256]{2,1,0:T(8,128)(2,1)S(1)} %copy-done.2, bf16[2,256,256]{2,1,0:T(8,128)(2,1)S(1)} %copy-done.1, bf16[2,128,128]{2,1,0:T(8,128)(2,1)S(1)} %copy-done.6, bf16[2,128,128]{2,1,0:T(8,128)(2,1)S(1)} %copy-done.5, ...), custom_call_target="tpu_custom_call" | custom-call | tf_op jit(solution)/shard_map/pallas_call | solution.py:423
  63.4 1.3 %copy.9 = f32[32,64,256]{2,1,0:T(8,128)} copy(f32[32,64,256]{2,1,0:T(8,128)S(1)} %shard_map.73) | data formatting | bytes 4194304
Async XLA Ops:
  0.0 1.6 %copy-start = (s32[32,64,256]{2,1,0:T(8,128)S(1)}, s32[32,64,256]{2,1,0:T(8,128)}, u32[]{:S(2)}) copy-start(s32[32,64,256]{2,1,0:T(8,128)} %counts.1) | copy-start | bytes 6291460
  1.6 0.9 %copy-start.1 = (bf16[2,256,256]{2,1,0:T(8,128)(2,1)S(1)}, bf16[2,256,256]{2,1,0:T(8,128)(2,1)}, u32[]{:S(2)}) copy-start(bf16[2,256,256]{2,1,0:T(8,128)(2,1)} %constant.13.clone.m1t) | copy-start | bytes 786436
  2.5 0.9 %copy-start.2 = (bf16[2,256,256]{2,1,0:T(8,128)(2,1)S(1)}, bf16[2,256,256]{2,1,0:T(8,128)(2,1)}, u32[]{:S(2)}) copy-start(bf16[2,256,256]{2,1,0:T(8,128)(2,1)} %constant.12.clone.m1) | copy-start | bytes 786436
  3.5 0.8 %copy-start.3 = (bf16[2,128,128]{2,1,0:T(8,128)(2,1)S(1)}, bf16[2,128,128]{2,1,0:T(8,128)(2,1)}, u32[]{:S(2)}) copy-start(bf16[2,128,128]{2,1,0:T(8,128)(2,1)} %constant.17.clone.m3t) | copy-start | bytes 196612
  4.3 0.8 %copy-start.4 = (bf16[2,128,128]{2,1,0:T(8,128)(2,1)S(1)}, bf16[2,128,128]{2,1,0:T(8,128)(2,1)}, u32[]{:S(2)}) copy-start(bf16[2,128,128]{2,1,0:T(8,128)(2,1)} %constant.16.clone.m3) | copy-start | bytes 196612
  5.2 0.8 %copy-start.5 = (bf16[2,128,128]{2,1,0:T(8,128)(2,1)S(1)}, bf16[2,128,128]{2,1,0:T(8,128)(2,1)}, u32[]{:S(2)}) copy-start(bf16[2,128,128]{2,1,0:T(8,128)(2,1)} %constant.15.clone.m2t) | copy-start | bytes 196612
  6.0 0.8 %copy-start.6 = (bf16[2,128,128]{2,1,0:T(8,128)(2,1)S(1)}, bf16[2,128,128]{2,1,0:T(8,128)(2,1)}, u32[]{:S(2)}) copy-start(bf16[2,128,128]{2,1,0:T(8,128)(2,1)} %constant.14.clone.m2) | copy-start | bytes 196612
where the time goes:
time: 65.1 us; the launch traced here: 64.7 us
  Pallas kernels  56.5 us (87%)
  local copies, waits for them, and re-layouts  8.17 us (13%)
    pallas_call x1, Pallas kernels, on_device(): pl.pallas_call(functools.partial(kernel, nx, ny), out_shape=jax.ShapeDtyp...  56.5 us
    unnamed x15, local copies, waits for them, and re-layouts  8.17 us

commit v1 on v0

--- a/solution.py
+++ b/solution.py
@@ -43,8 +43,7 @@
 def times(values, matrix_ref):
     high = values.astype(BF16)
     low = (values - high.astype(F32)).astype(BF16)
-    first = matrix_ref[0]
-    second = matrix_ref[1]
+    first, second = matrix_ref()
     dot = functools.partial(jnp.dot, preferred_element_type=F32)
     return dot(high, first) + (dot(low, first) + dot(high, second))
 
@@ -69,7 +68,7 @@
     return (H[1] * lo + G[1] * hi) + (H[3] * lo_before + G[3] * hi_before)
 
 
-def loop(count, body, unroll=1):
+def loop(count, body, unroll=4):
     def step(i, carry):
         body(i)
         return carry
@@ -83,14 +82,14 @@
 
 def kernel(
     nx, ny,
-    counts, m1, m1t, m2, m2t, m3, m3t, out,
+    counts_hbm, mats_hbm, out, counts, corner_counts, mats,
     t0, a0, c1, e1, t2, a2, c2, e2, t3, a3, c3,
-    s3, p3, d2, s2, p2, d1, s1, p1, reb, edge,
+    s3, p3, d2, s2, p2, d1, s1, p1, reb, edge, halo,
     f0x, f0y, f0c, f0xr, f0yr, f0cr,
     f1x, f1y, f1c, f1xr, f1yr, f1cr,
     i1x, i1y, i1c, i1xr, i1yr, i1cr,
     i2x, i2y, i2c, i2xr, i2yr, i2cr,
-    send_sem, recv_sem,
+    local_sem, send_sem, recv_sem,
 ):
     gx = lax.axis_index("gx")
     gy = lax.axis_index("gy")
@@ -98,6 +97,26 @@
     y_after, y_before = lax.rem(gy + 1, ny), lax.rem(gy + ny - 1, ny)
     before = [{"gx": x_before}, {"gy": y_before}, {"gx": x_before, "gy": y_before}]
     after = [{"gx": x_after}, {"gy": y_after}, {"gx": x_after, "gy": y_after}]
+
+    loads = [
+        pltpu.make_async_copy(source, target, local_sem.at[n])
+        for n, (source, target) in enumerate(
+            [
+                (counts_hbm.at[:, 0:8, :], corner_counts),
+                (counts_hbm.at[0:2], counts.at[0:2]),
+                (mats_hbm, mats),
+                (counts_hbm.at[2:32], counts.at[2:32]),
+            ]
+        )
+    ]
+    for load in loads:
+        load.start()
+
+    def matrix(first_row, size, first_column, width):
+        return [
+            mats[n, first_row : first_row + size, first_column : first_column + width]
+            for n in range(2)
+        ]
 
     barrier = pltpu.get_barrier_semaphore()
     for other in before + after:
@@ -135,6 +154,16 @@
         def old(ref, *index):
             return 0.0 if first else ref[index]
 
+        m1 = functools.partial(matrix, 0, 256, 0, 256)
+        m1t = functools.partial(matrix, 256, 256, 0, 256)
+        m2 = functools.partial(matrix, 512, 128, 0, 128)
+        m2t = functools.partial(matrix, 512, 128, 128, 128)
+        m3 = functools.partial(matrix, 640, 128, 0, 128)
+        m3t = functools.partial(matrix, 640, 128, 128, 128)
+
+        if first:
+            loads[0].wait()
+            loads[1].wait()
         for i in range(2):
             for th in range(2):
                 f0x[th, i * 64 : (i + 1) * 64, :] = residual(
@@ -145,7 +174,7 @@
         def edge_row(x):
             for th in range(2):
                 edge[th, rows(x * 8, 8), :] = residual(
-                    counts[x, 0:8, th * 128 : (th + 1) * 128],
+                    corner_counts[x, :, th * 128 : (th + 1) * 128],
                     None if first else reb[th, rows(x * 64, 8), :],
                 )
 
@@ -154,10 +183,15 @@
             for j in range(2):
                 f0y[th, j * 32 : (j + 1) * 32, :] = edge[th, pl.ds(j, 32, stride=8), :]
             for i in range(2):
-                f0c[th, i * 8 : (i + 1) * 8, :] = f0x[th, i * 64 : i * 64 + 8, :]
+                n = th * 8 + i * 4
+                f0c[n : n + 4, :] = f0x[th, i * 64 : i * 64 + 4, :]
         if first:
             pl.semaphore_wait(barrier, 6)
         f0 = send(4 * number, [f0x, f0y, f0c], [f0xr, f0yr, f0cr], before)
+
+        if first:
+            loads[2].wait()
+            loads[3].wait()
 
         def time_rows(n):
             count = counts[pl.ds(n * 4, 4)].reshape(256, 256)
@@ -189,11 +223,11 @@
                 t0[tb, pl.ds(64 + j, 32, stride=72), :] = result[
                     j * 32 : (j + 1) * 32, tb * 128 : (tb + 1) * 128
                 ]
-        result = times(jnp.concatenate([f0cr[0], f0cr[1]], axis=1), m1)
+        result = times(jnp.concatenate([f0cr[0:8], f0cr[8:16]], axis=1), m1)
         for i in range(2):
             for tb in range(2):
-                t0[tb, (32 + i) * 72 + 64 : (33 + i) * 72, :] = result[
-                    i * 8 : (i + 1) * 8, tb * 128 : (tb + 1) * 128
+                t0[tb, (32 + i) * 72 + 64 : (32 + i) * 72 + 66, :] = result[
+                    i * 4 : i * 4 + 2, tb * 128 : (tb + 1) * 128
                 ]
 
         def x_level1(k):
@@ -227,8 +261,19 @@
         for b in range(7):
             i1x[b * 32 : (b + 1) * 32, :] = c1[b, 16 * 40 + 8 : 17 * 40, :]
             i1y[b * 16 : (b + 1) * 16, :] = c1[b, pl.ds(40 + 39, 16, stride=40), :]
-            i1c[b * 8 : (b + 1) * 8, :] = c1[b, 16 * 40 + 32 : 17 * 40, :]
+            i1c[b : b + 1, :] = c1[b, 17 * 40 - 1 : 17 * 40, :]
+        i1c[7:8, :] = i1c[6:7, :]
         i1 = send(4 * number + 2, [i1x, i1y, i1c], [i1xr, i1yr, i1cr], after)
+
+        def time_up1_own(n):
+            place = rows(40 + n * 128, 128)
+            for b in range(1, 4):
+                values = jnp.concatenate([c1[2 * b - 1, place, :], c1[2 * b, place, :]], axis=1)
+                result = times(values, m1t)
+                s1[0, b, place, :] = result[:, :128]
+                s1[1, b, place, :] = result[:, 128:]
+
+        loop(5, time_up1_own)
         wait(f1)
         for i in range(6):
             e1[(16 + i) * 40 : (16 + i) * 40 + 32, :] = f1xr[i * 32 : (i + 1) * 32, :]
@@ -297,9 +342,39 @@
                 i2x[128 + n * 8 : 128 + (n + 1) * 8, :] = c3[b, (4 + i) * 16 + 8 : (5 + i) * 16, :]
                 i2y[n * 8 : (n + 1) * 8, :] = c2[b, pl.ds(2 * 24 + 22 + i, 8, stride=24), :]
                 i2y[64 + n * 4 : 64 + (n + 1) * 4, :] = c3[b, pl.ds(2 * 16 + 14 + i, 4, stride=16), :]
-                i2c[n * 8 : (n + 1) * 8, :] = c2[b, (8 + i) * 24 + 16 : (9 + i) * 24, :]
-                i2c[64 + n * 8 : 64 + (n + 1) * 8, :] = c3[b, (4 + i) * 16 + 8 : (5 + i) * 16, :]
+                i2c[n * 2 : n * 2 + 2, :] = c2[b, (9 + i) * 24 - 2 : (9 + i) * 24, :]
+                i2c[16 + n * 2 : 18 + n * 2, :] = c3[b, (5 + i) * 16 - 2 : (5 + i) * 16, :]
         i2 = send(4 * number + 3, [i2x, i2y, i2c], [i2xr, i2yr, i2cr], after)
+
+        wait(i1)
+        c1[0, 8:40, :] = i1xr[0:32, :]
+        c1[0, pl.ds(40 + 7, 16, stride=40), :] = i1yr[0:16, :]
+        c1[0, 7:8, :] = i1cr[0:1, :]
+        for b in range(1, 4):
+            n = (b - 1) * 56
+            for tb in range(2):
+                d = 2 * b - 1 + tb
+                halo[tb, n : n + 32, :] = i1xr[d * 32 : (d + 1) * 32, :]
+                halo[tb, n + 32 : n + 48, :] = i1yr[d * 16 : (d + 1) * 16, :]
+                halo[tb, n + 55 : n + 56, :] = i1cr[d : d + 1, :]
+        result = times(jnp.concatenate([halo[0], halo[1]], axis=1), m1t)
+        for b in range(1, 4):
+            n = (b - 1) * 56
+            for th in range(2):
+                part = result[n : n + 56, th * 128 : (th + 1) * 128]
+                s1[th, b, 8:40, :] = part[0:32]
+                s1[th, b, pl.ds(40 + 7, 16, stride=40), :] = part[32:48]
+                s1[th, b, 0:8, :] = part[48:56]
+
+        def x_up1(yb, k):
+            for th in range(2):
+                e = [s1[th, b, rows((k + d) * 40, 40), :] for d in (1, 0) for b in (yb, 2 + yb)]
+                p1[th, yb, rows(2 * k * 40, 40), :] = even_of(*e)
+                p1[th, yb, rows((2 * k + 1) * 40, 40), :] = odd_of(*e)
+
+        x_up1_low = functools.partial(x_up1, 0)
+        x_up1_high = functools.partial(x_up1, 1)
+        loop(16, x_up1_high)
         wait(i2)
         for b in range(4):
             for i in range(2):
@@ -308,8 +383,8 @@
                 c3[b, i * 16 + 8 : (i + 1) * 16, :] = i2xr[128 + n * 8 : 128 + (n + 1) * 8, :]
                 c2[b, pl.ds(2 * 24 + 6 + i, 8, stride=24), :] = i2yr[n * 8 : (n + 1) * 8, :]
                 c3[b, pl.ds(2 * 16 + 6 + i, 4, stride=16), :] = i2yr[64 + n * 4 : 64 + (n + 1) * 4, :]
-                c2[b, i * 24 : i * 24 + 8, :] = i2cr[n * 8 : (n + 1) * 8, :]
-                c3[b, i * 16 : i * 16 + 8, :] = i2cr[64 + n * 8 : 64 + (n + 1) * 8, :]
+                c2[b, i * 24 + 6 : i * 24 + 8, :] = i2cr[n * 2 : n * 2 + 2, :]
+                c3[b, i * 16 + 6 : i * 16 + 8, :] = i2cr[16 + n * 2 : 18 + n * 2, :]
 
         for b in range(4):
             s3[b] = times(c3[b], m3t)
@@ -349,31 +424,16 @@
 
         loop(18, y_up2)
 
-        wait(i1)
-        for b in range(7):
-            c1[b, 8:40, :] = i1xr[b * 32 : (b + 1) * 32, :]
-            c1[b, pl.ds(40 + 7, 16, stride=40), :] = i1yr[b * 16 : (b + 1) * 16, :]
-            c1[b, 0:8, :] = i1cr[b * 8 : (b + 1) * 8, :]
-
         def time_up1(n):
             place = rows(n * 136, 136)
-            for b in range(4):
-                lo = d1[rows(40 + n * 136, 136), :] if b == 0 else c1[2 * b - 1, place, :]
-                values = jnp.concatenate([lo, c1[2 * b, place, :]], axis=1)
-                result = times(values, m1t)
-                s1[0, b, place, :] = result[:, :128]
-                s1[1, b, place, :] = result[:, 128:]
+            lo = d1[rows(40 + n * 136, 136), :]
+            result = times(jnp.concatenate([lo, c1[0, place, :]], axis=1), m1t)
+            s1[0, 0, place, :] = result[:, :128]
+            s1[1, 0, place, :] = result[:, 128:]
 
         loop(5, time_up1)
 
-        def x_up1(k):
-            for th in range(2):
-                for yb in range(2):
-                    e = [s1[th, b, rows((k + d) * 40, 40), :] for d in (1, 0) for b in (yb, 2 + yb)]
-                    p1[th, yb, rows(2 * k * 40, 40), :] = even_of(*e)
-                    p1[th, yb, rows((2 * k + 1) * 40, 40), :] = odd_of(*e)
-
-        loop(16, x_up1)
+        loop(16, x_up1_low)
 
         def y_up1(r):
             for th in range(2):
@@ -399,37 +459,44 @@
     m2, m2t = time_matrices(128, 128)
     m3, m3t = time_matrices(64, 128)
 
+    mats = np.concatenate(
+        [m1, m1t, np.concatenate([m2, m2t], axis=2), np.concatenate([m3, m3t], axis=2)], axis=1
+    )
+
     def v(*shape):
         return pltpu.VMEM(shape, F32)
 
     scratch = [
+        pltpu.VMEM((32, 64, 256), jnp.int32), pltpu.VMEM((32, 8, 256), jnp.int32),
+        pltpu.VMEM(mats.shape, BF16),
         v(2, 34 * 72, 128), v(4, 16 * 72, 128), v(7, 17 * 40, 128), v(22 * 40, 128),
         v(22 * 40, 128), v(2, 10 * 40, 128), v(4, 10 * 24, 128), v(10 * 24, 128),
         v(10 * 24, 128), v(2, 4 * 24, 128), v(4, 6 * 16, 128),
         v(4, 6 * 16, 128), v(2, 10 * 16, 128), v(10 * 24, 128),
         v(4, 10 * 24, 128), v(2, 18 * 24, 128), v(18 * 40, 128),
         v(2, 4, 17 * 40, 128), v(2, 2, 32 * 40, 128), v(2, 32 * 64, 128), v(2, 32 * 8, 128),
+        v(2, 168, 128),
     ]
     for shapes in (
-        ((2, 128, 128), (2, 64, 128), (2, 16, 128)),
+        ((2, 128, 128), (2, 64, 128), (16, 128)),
         ((192, 128), (96, 128), (48, 128)),
-        ((224, 128), (112, 128), (56, 128)),
-        ((192, 128), (96, 128), (128, 128)),
+        ((224, 128), (112, 128), (8, 128)),
+        ((192, 128), (96, 128), (32, 128)),
     ):
         scratch += [v(*shape) for shape in shapes] * 2
-    scratch += [pltpu.SemaphoreType.DMA((24,)), pltpu.SemaphoreType.DMA((24,))]
+    scratch += [pltpu.SemaphoreType.DMA((4,)), pltpu.SemaphoreType.DMA((24,)), pltpu.SemaphoreType.DMA((24,))]
 
     def on_device(counts):
         return pl.pallas_call(
             functools.partial(kernel, nx, ny),
             out_shape=jax.ShapeDtypeStruct(counts.shape, F32),
-            in_specs=[pl.BlockSpec(memory_space=pltpu.VMEM)] * 7,
+            in_specs=[pl.BlockSpec(memory_space=pltpu.HBM)] * 2,
             out_specs=pl.BlockSpec(memory_space=pltpu.VMEM),
             scratch_shapes=scratch,
             compiler_params=pltpu.CompilerParams(
-                collective_id=0, has_side_effects=True, vmem_limit_bytes=48 * 1024 * 1024
+                collective_id=0, has_side_effects=True, vmem_limit_bytes=60 * 1024 * 1024
             ),
-        )(counts, m1, m1t, m2, m2t, m3, m3t)
+        )(counts, mats)
 
     spec = P(("grp", "gx"), "gy", None)
     return jax.shard_map(on_device, mesh=mesh, in_specs=(spec,), out_specs=spec, check_vma=False)

time: 65.1 us -> 52.7 us (0.81)
  Pallas kernels: 56.5 us -> 49.4 us
  local copies, waits for them, and re-layouts: 8.17 us -> 3.13 us
    pallas_call x1, Pallas kernels: 56.5 us -> 49.4 us  [on_device(): pl.pallas_call(functools.partial(kernel, nx, ny), out_shape=jax.ShapeDtyp...]
    unnamed x15 -> x1, local copies, waits for them, and re-layouts: 8.17 us -> 3.13 us
where the time goes in v1:
time: 52.7 us; the launch traced here: 52.5 us
  Pallas kernels  49.4 us (94%)
  local copies, waits for them, and re-layouts  3.13 us (6%)
    pallas_call x1, Pallas kernels, on_device(): pl.pallas_call(functools.partial(kernel, nx, ny), out_shape=jax.ShapeDtyp...  49.4 us
    unnamed x1, local copies, waits for them, and re-layouts  3.13 us

profile of v1, /device:TPU:0, one launch (start us, length us, event | category | flops | bytes accessed | tf_op | source)
XLA Modules:
  0.0 52.5 jit_solution(12465535710493785112)
XLA Ops:
  0.0 49.4 %shard_map.28 = f32[32,64,256]{2,1,0:T(8,128)} custom-call(s32[32,64,256]{2,1,0:T(8,128)} %counts_hbm.1, bf16[2,768,256]{2,1,0:T(8,128)(2,1)} %constant.2.clone.mats_hbm), custom_call_target="tpu_custom_call" | custom-call | tf_op jit(solution)/shard_map/pallas_call | solution.py:490
  49.4 3.1 %copy.4 = f32[32,64,256]{2,1,0:T(8,128)} copy(f32[32,64,256]{2,1,0:T(8,128)} %shard_map.28) | data formatting | bytes 4194304

commit v2 on v1

--- a/solution.py
+++ b/solution.py
@@ -494,7 +494,7 @@
             out_specs=pl.BlockSpec(memory_space=pltpu.VMEM),
             scratch_shapes=scratch,
             compiler_params=pltpu.CompilerParams(
-                collective_id=0, has_side_effects=True, vmem_limit_bytes=60 * 1024 * 1024
+                collective_id=0, has_side_effects=True, vmem_limit_bytes=50 * 1024 * 1024
             ),
         )(counts, mats)
 

time: 52.7 us -> 50.7 us (0.962)
  Pallas kernels: 49.4 us -> 48.1 us
  local copies, waits for them, and re-layouts: 3.13 us -> 2.45 us
    pallas_call x1, Pallas kernels: 49.4 us -> 48.1 us  [on_device(): pl.pallas_call(functools.partial(kernel, nx, ny), out_shape=jax.ShapeDtyp...]
    unnamed x1 -> x3, local copies, waits for them, and re-layouts: 3.13 us -> 2.45 us
where the time goes in v2:
time: 50.7 us; the launch traced here: 50.6 us
  Pallas kernels  48.1 us (95%)
  local copies, waits for them, and re-layouts  2.45 us (5%)
    pallas_call x1, Pallas kernels, on_device(): pl.pallas_call(functools.partial(kernel, nx, ny), out_shape=jax.ShapeDtyp...  48.1 us
    unnamed x3, local copies, waits for them, and re-layouts  2.45 us

profile of v2, /device:TPU:0, one launch (start us, length us, event | category | flops | bytes accessed | tf_op | source)
XLA Modules:
  0.0 50.6 jit_solution(10311630596811144834)
XLA Ops:
  0.0 0.0 copy-start
  0.0 1.1 %copy-done = bf16[2,768,256]{2,1,0:T(8,128)(2,1)S(1)} copy-done((bf16[2,768,256]{2,1,0:T(8,128)(2,1)S(1)}, bf16[2,768,256]{2,1,0:T(8,128)(2,1)}, u32[]{:S(2)}) %copy-start) | copy-done | bytes 786456
  1.1 48.1 %shard_map.28 = f32[32,64,256]{2,1,0:T(8,128)S(1)} custom-call(s32[32,64,256]{2,1,0:T(8,128)} %counts_hbm.1, bf16[2,768,256]{2,1,0:T(8,128)(2,1)S(1)} %copy-done), custom_call_target="tpu_custom_call" | custom-call | tf_op jit(solution)/shard_map/pallas_call | solution.py:490
  49.3 1.3 %copy.4 = f32[32,64,256]{2,1,0:T(8,128)} copy(f32[32,64,256]{2,1,0:T(8,128)S(1)} %shard_map.28) | data formatting | bytes 4194304
Async XLA Ops:
  0.0 1.1 %copy-start = (bf16[2,768,256]{2,1,0:T(8,128)(2,1)S(1)}, bf16[2,768,256]{2,1,0:T(8,128)(2,1)}, u32[]{:S(2)}) copy-start(bf16[2,768,256]{2,1,0:T(8,128)(2,1)} %constant.2.clone.mats_hbm) | copy-start | bytes 2359300
